TPU v7x, 512 devices: a whole 4x8x8 slice. The times are simulated.
512 devices in a mesh: expert: 64 (over x, z, core), replica: 8 (over y).
Axes of the slice: x: 4, y: 8, z: 8, core: 2. Of those that a mesh axis runs over, the one named last changes fastest.
Arguments:
- tokens: bfloat16 [768, 3584], P('expert', 'replica'), may hold values from -6 to 6
- expert_ids: int32 [768, 8], P('expert'), may hold values from 0 to 31, all different within a row; in each aligned block of 12 rows (0 to 11, 12 to 23, ...) at most 4 rows name the same one
- gate_values: float32 [768, 8], P('expert'), may hold values from 0.1 to 0.6
- gate_weight: bfloat16 [64, 512, 3584], P('expert', 'replica'), may hold values from -0.09375 to 0.09375
- up_weight: bfloat16 [64, 512, 3584], P('expert', 'replica'), may hold values from -0.09375 to 0.09375
- down_weight: bfloat16 [64, 512, 3584], P('expert', None, 'replica'), may hold values from -0.1875 to 0.1875
- out_grad: bfloat16 [768, 3584], P('expert', 'replica'), may hold values from -1.5 to 1.5
Outputs:
- moe_out: bfloat16 [768, 3584], P('expert', 'replica')
- token_grad: bfloat16 [768, 3584], P('expert', 'replica')
- gate_grad: bfloat16 [64, 512, 3584], P('expert', 'replica')
- up_grad: bfloat16 [64, 512, 3584], P('expert', 'replica')
- down_grad: bfloat16 [64, 512, 3584], P('expert', None, 'replica')
Inputs may be any that keep to these rules, and one draw needn't show every extreme that they name: `expert_ids`: each row names 8 different experts. Among the 12 rows of one index of expert, no expert is named by more than 4 rows, a bound that some block reaches.
All inputs are finite; a program needn't handle non-finite values.
Results may differ from a plain program's by a relative error of at most 0.0075.
Values may be sent and summed in bfloat16 or wider, within the bound.
A program may use at most 64 MiB of HBM per device.

v0:
```python
import jax
import jax.numpy as jnp
from jax import lax
from jax.sharding import PartitionSpec as P


def partner_2(block, axis, distance):
    count = lax.axis_size(axis)
    route = []
    for low in range(count):
        high = low | 1 << distance
        if high != low and high < count:
            route += [(low, high), (high, low)]
    return lax.ppermute(block, axis, route)


def pair_join(parity_bit, own_part, peer_part, stack_axis):
    first_part = jnp.where(parity_bit == 0, own_part, peer_part)
    second_part = jnp.where(parity_bit == 0, peer_part, own_part)
    return jnp.stack([first_part, second_part], axis=stack_axis)


def pick_half(parity_bit, stacked, stack_axis):
    lower = jnp.take(stacked, 0, axis=stack_axis)
    higher = jnp.take(stacked, 1, axis=stack_axis)
    return (jnp.where(parity_bit == 0, lower, higher), jnp.where(parity_bit == 0, higher, lower))


def per_device(tokens, expert_ids, gate_values, gate_weight, up_weight, down_weight, out_grad):
    experts_axis = lax.axis_size("expert")
    tok_rows, slice_width = tokens.shape
    top_count = expert_ids.shape[1]
    expert_count = experts_axis // 2
    most_rows = min(tok_rows, 4 * tok_rows * top_count // (3 * expert_count))
    capacity = (most_rows + 1) // 2
    pair_count = tok_rows * top_count
    slot_count = experts_axis * capacity
    flat_ids = expert_ids.reshape(pair_count)
    onehot = (flat_ids[:, None] == jnp.arange(expert_count, dtype=jnp.int32)[None, :]).astype(
        jnp.int32
    )
    rank_in = jnp.sum((jnp.cumsum(onehot, axis=0) - onehot) * onehot, axis=1)
    upper_copy = (rank_in >= capacity).astype(jnp.int32)
    target = (2 * flat_ids + upper_copy) * capacity + rank_in - upper_copy * capacity
    slot_match = target[None, :] == jnp.arange(slot_count, dtype=jnp.int32)[:, None]
    filled = jnp.any(slot_match, axis=1)
    source_pair = jnp.sum(
        jnp.where(slot_match, jnp.arange(pair_count, dtype=jnp.int32)[None, :], 0), axis=1
    )
    source_token = source_pair // top_count
    flat_gates = gate_values.reshape(pair_count)
    send_rows = jnp.where(filled[:, None], tokens[source_token], jnp.zeros((), tokens.dtype))
    scaled = flat_gates[source_pair][:, None] * out_grad[source_token].astype(jnp.float32)
    send_grads = jnp.where(filled[:, None], scaled, 0.0).astype(jnp.bfloat16)
    got_rows, got_grads = (
        lax.all_to_all(
            send_rows.reshape(experts_axis, capacity, slice_width),
            "expert",
            split_axis=0,
            concat_axis=0,
            tiled=True,
        ),
        lax.all_to_all(
            send_grads.reshape(experts_axis, capacity, slice_width),
            "expert",
            split_axis=0,
            concat_axis=0,
            tiled=True,
        ),
    )
    rows_part = got_rows.reshape(slot_count, slice_width)
    grads_part = got_grads.reshape(slot_count, slice_width)
    parity_bit = lax.axis_index("expert") % 2
    own_pieces = (gate_weight[0], up_weight[0], down_weight[0])
    partner = partner_2((own_pieces[0], own_pieces[1], own_pieces[2]), "expert", 0)
    w_gate = pair_join(parity_bit, own_pieces[0], partner[0], 0)
    w_up = pair_join(parity_bit, own_pieces[1], partner[1], 0)
    w_down = pair_join(parity_bit, own_pieces[2], partner[2], 0)
    _, quarter, model_width = w_gate.shape
    full_rows = lax.all_gather(rows_part, "replica", axis=1, tiled=True)
    contract = (((1,), (1,)), ((), ()))
    pre_gate = lax.dot_general(
        full_rows,
        w_gate.reshape(2 * quarter, model_width),
        contract,
        preferred_element_type=jnp.float32,
    ).reshape(slot_count, 2, quarter)
    pre_up = lax.dot_general(
        full_rows,
        w_up.reshape(2 * quarter, model_width),
        contract,
        preferred_element_type=jnp.float32,
    ).reshape(slot_count, 2, quarter)
    sigma = jax.nn.sigmoid(pre_gate)
    activated = pre_gate * sigma
    slope_term = sigma * (1.0 + pre_gate * (1.0 - sigma))
    hidden = (activated * pre_up).astype(jnp.bfloat16)
    all_hidden = lax.all_gather(hidden, "replica", axis=2, tiled=True).reshape(slot_count, -1)
    down_full = w_down.reshape(-1, slice_width)
    expert_out = jnp.dot(all_hidden, down_full, preferred_element_type=jnp.float32).astype(
        jnp.bfloat16
    )
    returned = lax.all_to_all(
        expert_out.reshape(experts_axis, capacity, slice_width),
        "expert",
        split_axis=0,
        concat_axis=0,
        tiled=True,
    ).reshape(slot_count, slice_width)
    picked = returned[target].astype(jnp.float32).reshape(tok_rows, top_count, slice_width)
    moe_out = jnp.sum(picked * gate_values[:, :, None], axis=1).astype(jnp.bfloat16)
    down_local = lax.dot_general(
        all_hidden, grads_part, (((0,), (0,)), ((), ())), preferred_element_type=jnp.float32
    )
    full_grads = lax.all_gather(grads_part, "replica", axis=1, tiled=True)
    down_rows = lax.all_to_all(w_down, "replica", split_axis=1, concat_axis=2, tiled=True)
    hidden_grad = jnp.einsum(
        "sd,hqd->shq", full_grads, down_rows, preferred_element_type=jnp.float32
    )
    gate_act = (hidden_grad * pre_up * slope_term).astype(jnp.bfloat16)
    up_act = (hidden_grad * activated).astype(jnp.bfloat16)
    gate_local = jnp.einsum("sd,shq->hqd", full_rows, gate_act, preferred_element_type=jnp.float32)
    up_local = jnp.einsum("sd,shq->hqd", full_rows, up_act, preferred_element_type=jnp.float32)
    all_gate_act, all_up_act = (
        lax.all_gather(gate_act, "replica", axis=2, tiled=True),
        lax.all_gather(up_act, "replica", axis=2, tiled=True),
    )
    rows_gate, rows_up = (
        lax.all_to_all(w_gate, "replica", split_axis=2, concat_axis=1, tiled=True),
        lax.all_to_all(w_up, "replica", split_axis=2, concat_axis=1, tiled=True),
    )
    input_rows = jnp.einsum(
        "shf,hfd->sd", all_gate_act, rows_gate, preferred_element_type=jnp.float32
    )
    input_rows = input_rows + jnp.einsum(
        "shf,hfd->sd", all_up_act, rows_up, preferred_element_type=jnp.float32
    )
    grads_back = lax.all_to_all(
        input_rows.astype(jnp.bfloat16).reshape(experts_axis, capacity, slice_width),
        "expert",
        split_axis=0,
        concat_axis=0,
        tiled=True,
    ).reshape(slot_count, slice_width)
    token_grad = jnp.sum(
        grads_back[target].astype(jnp.float32).reshape(tok_rows, top_count, slice_width), axis=1
    ).astype(jnp.bfloat16)
    keep_gate, give_gate = pick_half(parity_bit, gate_local, 0)
    keep_up, give_up = pick_half(parity_bit, up_local, 0)
    keep_down, give_down = pick_half(parity_bit, down_local.reshape(2, -1, slice_width), 0)
    received = (
        partner_2(give_gate.astype(jnp.bfloat16), "expert", 0).astype(give_gate.dtype),
        partner_2(give_up.astype(jnp.bfloat16), "expert", 0).astype(give_up.dtype),
        partner_2(give_down.astype(jnp.bfloat16), "expert", 0).astype(give_down.dtype),
    )
    gate_grad = (keep_gate + received[0]).astype(jnp.bfloat16)[None]
    up_grad = (keep_up + received[1]).astype(jnp.bfloat16)[None]
    down_grad = (keep_down + received[2]).astype(jnp.bfloat16)[None]
    return (moe_out, token_grad, gate_grad, up_grad, down_grad)


def solution(mesh):
    placed = (
        P("expert", "replica"),
        P("expert", None),
        P("expert", None),
        P("expert", "replica", None),
        P("expert", "replica", None),
        P("expert", None, "replica"),
        P("expert", "replica"),
    )
    return jax.shard_map(
        per_device,
        mesh=mesh,
        in_specs=placed,
        out_specs=(
            P("expert", "replica"),
            P("expert", "replica"),
            P("expert", "replica", None),
            P("expert", "replica", None),
            P("expert", None, "replica"),
        ),
        check_vma=False,
    )
```

profile of v0, /device:TPU:1, one launch (start us, length us, event | category | flops | bytes accessed | tf_op | source)
XLA Modules:
  0.0 322.7 jit_solution(3056633494185465903)
XLA Ops:
  0.7 8.9 %collective-permute-start.2 = (bf16[512,448]{0,1:T(8,128)(2,1)}, bf16[512,448]{0,1:T(8,128)(2,1)S(1)}, u32[]{:S(2)}, u32[]{:S(2)}) collective-permute-start(bf16[512,448]{0,1:T(8,128)(2,1)} %bitcast.169), channel_id=1, source_target_pairs={{0,8},{8,0},{16,24},{24,16},{32,40},{40,32},{48,56},{56,48},{64,72... | collective-permute-start | bytes 1376264 | tf_op jit(solution)/shard_map/ppermute | solution.py:14
  9.6 0.8 copy.56
  11.1 0.8 gather_fusion.3
  12.3 0.8 copy.60
  13.2 0.5 copy-done.18
  13.7 1.2 gather_fusion.2
  15.1 0.9 select_convert_fusion.3
  15.9 8.1 %all-to-all-start.2 = ((bf16[64,2,448]{2,1,0:T(2,128)(2,1)}), bf16[64,2,448]{2,1,0:T(2,128)(2,1)S(1)}, u32[]{:S(2)}, u32[]{:S(2)}) async-start(bf16[64,2,448]{2,1,0:T(2,128)(2,1)} %select_convert_fusion.3), calls=%async_computation.2 | async-start | bytes 262144 | tf_op jit(solution)/shard_map/all_to_all | solution.py:63
  24.0 2.4 collective-permute-start.1
  26.4 2.0 collective-permute-start
  28.4 0.8 gather_fusion
  29.5 0.9 broadcast_select_fusion
  30.4 4.0 %all-to-all-done.2 = bf16[64,2,448]{2,1,0:T(2,128)(2,1)S(1)} async-done(((bf16[64,2,448]{2,1,0:T(2,128)(2,1)}), bf16[64,2,448]{2,1,0:T(2,128)(2,1)S(1)}, u32[]{:S(2)}, u32[]{:S(2)}) %all-to-all-start.2) | async-done | bytes 114720 | tf_op jit(solution)/shard_map/all_to_all | solution.py:63
  34.4 6.3 %all-to-all-start = ((bf16[64,2,448]{2,1,0:T(2,128)(2,1)}), bf16[64,2,448]{2,1,0:T(2,128)(2,1)S(1)}, u32[]{:S(2)}, u32[]{:S(2)}) async-start(bf16[64,2,448]{2,1,0:T(2,128)(2,1)} %broadcast_select_fusion), calls=%async_computation | async-start | bytes 262144 | tf_op jit(solution)/shard_map/all_to_all | solution.py:56
  40.7 0.6 pad_clamp_fusion.1
  41.6 9.5 %all-to-all-done = bf16[64,2,448]{2,1,0:T(2,128)(2,1)S(1)} async-done(((bf16[64,2,448]{2,1,0:T(2,128)(2,1)}), bf16[64,2,448]{2,1,0:T(2,128)(2,1)S(1)}, u32[]{:S(2)}, u32[]{:S(2)}) %all-to-all-start) | async-done | bytes 114720 | tf_op jit(solution)/shard_map/all_to_all | solution.py:56
  51.3 24.1 %all_gather.17 = bf16[128,3584]{0,1:T(8,128)(2,1)} all-gather(bf16[128,448]{0,1:T(8,128)(2,1)S(1)} %copy.62), channel_id=1, replica_groups=mesh['expert'=64,'replica'=8] {'replica'}, dimensions={1}, use_global_device_ids=true | all-gather | bytes 1032192 | tf_op jit(solution)/shard_map/all_gather | solution.py:115
  75.6 2.1 copy.63
  77.7 6.0 %all-to-all-start.3 = ((bf16[2,512,448]{2,0,1:T(2,128)(2,1)}), bf16[2,512,448]{2,0,1:T(2,128)(2,1)}, u32[]{:S(2)}, u32[]{:S(2)}) async-start(bf16[2,512,448]{2,0,1:T(2,128)(2,1)} %copy.63), calls=%async_computation.3 | async-start | bytes 2097152 | tf_op jit(solution)/shard_map/all_to_all | solution.py:116
  83.7 41.3 %all_gather.15 = bf16[128,3584]{0,1:T(8,128)(2,1)S(1)} all-gather(bf16[128,448]{0,1:T(8,128)(2,1)S(1)} %copy.57), channel_id=1, replica_groups=mesh['expert'=64,'replica'=8] {'replica'}, dimensions={1}, use_global_device_ids=true | all-gather | bytes 1032192 | tf_op jit(solution)/shard_map/all_gather | solution.py:80
  125.0 1.1 select_bitcast_fusion.3
  126.1 0.7 copy-done.12
  127.0 1.0 pad_maximum_fusion.2
  128.0 4.3 %copy.69 = bf16[2,64,3584]{1,0,2:T(2,128)(2,1)S(1)} copy(bf16[2,64,3584]{2,1,0:T(8,128)(2,1)} %pad_maximum_fusion.2) | data formatting | bytes 1835008 | tf_op jit(solution)/shard_map/stack | solution.py:20
  132.3 2.1 reshape.363
  134.4 4.2 %all-to-all-start.5 = ((bf16[8,2,28672]{2,1,0:T(2,128)(2,1)}), bf16[8,2,28672]{2,1,0:T(2,128)(2,1)}, u32[]{:S(2)}, u32[]{:S(2)}) async-start(bf16[8,2,28672]{2,1,0:T(2,128)(2,1)} %reshape.363), calls=%async_computation.5 | async-start | bytes 1835008 | tf_op jit(solution)/shard_map/all_to_all | solution.py:130
  138.7 1.2 select_bitcast_fusion.5
  139.9 0.8 copy-done.8
  140.8 1.0 pad_maximum_fusion.1
  141.9 4.3 %copy.66 = bf16[2,64,3584]{1,0,2:T(2,128)(2,1)S(1)} copy(bf16[2,64,3584]{2,1,0:T(8,128)(2,1)} %pad_maximum_fusion.1) | data formatting | bytes 1835008 | tf_op jit(solution)/shard_map/stack | solution.py:20
  146.1 2.1 reshape.365
  148.3 2.2 fusion.9
  150.4 1.4 copy.64
  151.8 0.6 copy.65
  152.4 2.1 all_to_all.57
  154.5 6.7 %all-to-all-start.4 = ((bf16[8,2,28672]{2,1,0:T(2,128)(2,1)}), bf16[8,2,28672]{2,1,0:T(2,128)(2,1)}, u32[]{:S(2)}, u32[]{:S(2)}) async-start(bf16[8,2,28672]{2,1,0:T(2,128)(2,1)} %reshape.365), calls=%async_computation.4 | async-start | bytes 1835008 | tf_op jit(solution)/shard_map/all_to_all | solution.py:129
  161.6 0.6 copy-done.9
  162.8 30.9 %all_gather.16 = bf16[128,2,512]{0,2,1:T(8,128)(2,1)S(1)} all-gather(bf16[128,2,64]{0,2,1:T(8,128)(2,1)S(1)} %get-tuple-element.61), channel_id=1, replica_groups=mesh['expert'=64,'replica'=8] {'replica'}, dimensions={2}, use_global_device_ids=true | all-gather | bytes 294912 | tf_op jit(solution)/shard_map/all_gather | solution.py:98
  194.3 0.7 reshape.212
  195.1 4.5 %reshape.364 = bf16[3584,2,64]{2,1,0:T(2,128)(2,1)S(1)} reshape(bf16[8,2,28672]{2,1,0:T(2,128)(2,1)} %all-to-all-done.5) | data formatting | bytes 1835008
  199.6 3.5 %copy.70 = bf16[2,64,8,448]{3,1,2,0:T(8,128)(2,1)} copy(bf16[2,64,8,448]{1,0,3,2:T(2,128)(2,1)S(1)} %bitcast.164) | data formatting | bytes 1835008 | tf_op jit(solution)/shard_map/all_to_all | solution.py:130
  203.1 18.4 %all_gather.19 = bf16[128,2,512]{0,2,1:T(8,128)(2,1)S(1)} all-gather(bf16[128,2,64]{0,2,1:T(8,128)(2,1)S(1)} %get-tuple-element.60), channel_id=1, replica_groups=mesh['expert'=64,'replica'=8] {'replica'}, dimensions={2}, use_global_device_ids=true | all-gather | bytes 294912 | tf_op jit(solution)/shard_map/all_gather | solution.py:126
  221.5 18.8 %all_gather.18 = bf16[128,2,512]{0,2,1:T(8,128)(2,1)S(1)} all-gather(bf16[128,2,64]{0,2,1:T(8,128)(2,1)S(1)} %get-tuple-element.59), channel_id=1, replica_groups=mesh['expert'=64,'replica'=8] {'replica'}, dimensions={2}, use_global_device_ids=true | all-gather | bytes 294912 | tf_op jit(solution)/shard_map/all_gather | solution.py:125
  240.3 1.7 fusion.7
  242.3 27.9 %all-to-all-start.1 = ((bf16[64,2,448]{2,1,0:T(2,128)(2,1)}), bf16[64,2,448]{2,1,0:T(2,128)(2,1)S(1)}, u32[]{:S(2)}, u32[]{:S(2)}) async-start(bf16[64,2,448]{2,1,0:T(2,128)(2,1)} %reshape.212), calls=%async_computation.1 | async-start | bytes 262144 | tf_op jit(solution)/shard_map/all_to_all | solution.py:103
  270.2 5.3 %reshape.366 = bf16[3584,2,64]{2,1,0:T(2,128)(2,1)} reshape(bf16[8,2,28672]{2,1,0:T(2,128)(2,1)} %all-to-all-done.4) | data formatting | bytes 1835008
  275.5 5.8 %copy.67 = bf16[2,64,8,448]{3,1,2,0:T(8,128)(2,1)} copy(bf16[2,64,8,448]{1,0,3,2:T(2,128)(2,1)} %bitcast.165) | data formatting | bytes 1835008 | tf_op jit(solution)/shard_map/all_to_all | solution.py:129
  281.3 1.8 convolution_bitcast_fusion.1
  283.8 0.7 reshape.216
  284.6 2.3 select_convert_fusion.2
  286.9 2.4 collective-permute-start.3
  289.3 2.0 collective-permute-start.4
  291.3 1.7 fusion.16
  293.0 10.3 %all-to-all-start.6 = ((bf16[64,2,448]{2,1,0:T(2,128)(2,1)}), bf16[64,2,448]{2,1,0:T(2,128)(2,1)S(1)}, u32[]{:S(2)}, u32[]{:S(2)}) async-start(bf16[64,2,448]{2,1,0:T(2,128)(2,1)} %reshape.216), calls=%async_computation.6 | async-start | bytes 262144 | tf_op jit(solution)/shard_map/all_to_all | solution.py:138
  303.3 1.5 select_convert_fusion
  304.8 2.4 collective-permute-start.5
  307.3 0.9 gather_fusion.1
  308.2 5.4 %all-to-all-done.6 = bf16[64,2,448]{2,1,0:T(2,128)(2,1)S(1)} async-done(((bf16[64,2,448]{2,1,0:T(2,128)(2,1)}), bf16[64,2,448]{2,1,0:T(2,128)(2,1)S(1)}, u32[]{:S(2)}, u32[]{:S(2)}) %all-to-all-start.6) | async-done | bytes 114720 | tf_op jit(solution)/shard_map/all_to_all | solution.py:138
  313.8 0.9 gather_fusion.4
  314.7 0.7 bitcast_reduce_fusion
  315.3 0.7 fusion.18
  316.1 2.5 fusion.13
  318.6 2.0 fusion.14
  320.6 2.1 fusion.15
  (84 shorter events, 5.5 us)
Async XLA Ops:
  0.6 10.5 %copy-start = (bf16[12,448]{1,0:T(8,128)(2,1)S(1)}, bf16[12,448]{1,0:T(8,128)(2,1)}, u32[]{:S(2)}) copy-start(bf16[12,448]{1,0:T(8,128)(2,1)} %param.21) | copy-start | bytes 32260
  0.6 27.7 %copy-start.20 = (s32[12,8]{0,1:T(8,128)S(1)}, s32[12,8]{0,1:T(8,128)}, u32[]{:S(2)}) copy-start(s32[12,8]{0,1:T(8,128)} %param.16) | copy-start | bytes 1156
  0.7 23.4 %copy-start.17 = (bf16[1,64,3584]{2,1,0:T(8,128)(2,1)S(1)}, bf16[1,64,3584]{2,1,0:T(8,128)(2,1)}, u32[]{:S(2)}) copy-start(bf16[1,64,3584]{2,1,0:T(8,128)(2,1)} %param.19) | copy-start | bytes 1376260
  0.7 27.7 %copy-start.1 = (bf16[12,448]{1,0:T(8,128)(2,1)S(1)}, bf16[12,448]{1,0:T(8,128)(2,1)}, u32[]{:S(2)}) copy-start(bf16[12,448]{1,0:T(8,128)(2,1)} %param.15) | copy-start | bytes 32260
  0.7 74.7 %collective-permute-start.2 = (bf16[512,448]{0,1:T(8,128)(2,1)}, bf16[512,448]{0,1:T(8,128)(2,1)S(1)}, u32[]{:S(2)}, u32[]{:S(2)}) collective-permute-start(bf16[512,448]{0,1:T(8,128)(2,1)} %bitcast.169), channel_id=1, source_target_pairs={{0,8},{8,0},{16,24},{24,16},{32,40},{40,32},{48,56},{56,48},{64,72... | collective-permute-start | bytes 1376264 | tf_op jit(solution)/shard_map/ppermute | solution.py:14
  13.1 0.6 copy-start.18
  15.9 18.4 %all-to-all-start.2 = ((bf16[64,2,448]{2,1,0:T(2,128)(2,1)}), bf16[64,2,448]{2,1,0:T(2,128)(2,1)S(1)}, u32[]{:S(2)}, u32[]{:S(2)}) async-start(bf16[64,2,448]{2,1,0:T(2,128)(2,1)} %select_convert_fusion.3), calls=%async_computation.2 | async-start | bytes 262144 | tf_op jit(solution)/shard_map/all_to_all | solution.py:63
  24.0 101.0 %collective-permute-start.1 = (bf16[64,3584]{1,0:T(8,128)(2,1)S(1)}, bf16[64,3584]{1,0:T(8,128)(2,1)}, u32[]{:S(2)}, u32[]{:S(2)}) collective-permute-start(bf16[64,3584]{1,0:T(8,128)(2,1)S(1)} %bitcast.170), channel_id=1, source_target_pairs={{0,8},{8,0},{16,24},{24,16},{32,40},{40,32},{48,56},{56,48},{64,72... | collective-permute-start | bytes 1376264 | tf_op jit(solution)/shard_map/ppermute | solution.py:14
  26.4 112.3 %collective-permute-start = (bf16[64,3584]{1,0:T(8,128)(2,1)}, bf16[64,3584]{1,0:T(8,128)(2,1)}, u32[]{:S(2)}, u32[]{:S(2)}) collective-permute-start(bf16[64,3584]{1,0:T(8,128)(2,1)} %bitcast.3), channel_id=1, source_target_pairs={{0,8},{8,0},{16,24},{24,16},{32,40},{40,32},{48,56},{56,48},{64,72... | collective-permute-start | bytes 1376264 | tf_op jit(solution)/shard_map/ppermute | solution.py:14
  28.4 47.0 %copy-start.16 = (bf16[1,512,448]{1,2,0:T(8,128)(2,1)S(1)}, bf16[1,512,448]{1,2,0:T(8,128)(2,1)}, u32[]{:S(2)}) copy-start(bf16[1,512,448]{1,2,0:T(8,128)(2,1)} %param.20) | copy-start | bytes 1376260
  34.4 16.7 %all-to-all-start = ((bf16[64,2,448]{2,1,0:T(2,128)(2,1)}), bf16[64,2,448]{2,1,0:T(2,128)(2,1)S(1)}, u32[]{:S(2)}, u32[]{:S(2)}) async-start(bf16[64,2,448]{2,1,0:T(2,128)(2,1)} %broadcast_select_fusion), calls=%async_computation | async-start | bytes 262144 | tf_op jit(solution)/shard_map/all_to_all | solution.py:56
  75.5 2.2 copy-start.6
  77.7 56.7 %all-to-all-start.3 = ((bf16[2,512,448]{2,0,1:T(2,128)(2,1)}), bf16[2,512,448]{2,0,1:T(2,128)(2,1)}, u32[]{:S(2)}, u32[]{:S(2)}) async-start(bf16[2,512,448]{2,0,1:T(2,128)(2,1)} %copy.63), calls=%async_computation.3 | async-start | bytes 2097152 | tf_op jit(solution)/shard_map/all_to_all | solution.py:116
  126.1 0.8 copy-start.12
  126.1 0.9 copy-start.13
  134.4 20.1 %all-to-all-start.5 = ((bf16[8,2,28672]{2,1,0:T(2,128)(2,1)}), bf16[8,2,28672]{2,1,0:T(2,128)(2,1)}, u32[]{:S(2)}, u32[]{:S(2)}) async-start(bf16[8,2,28672]{2,1,0:T(2,128)(2,1)} %reshape.363), calls=%async_computation.5 | async-start | bytes 1835008 | tf_op jit(solution)/shard_map/all_to_all | solution.py:130
  139.9 0.8 copy-start.8
  139.9 0.9 copy-start.10
  152.4 8.8 %copy-start.4 = (bf16[128,3584]{0,1:T(8,128)(2,1)S(1)}, bf16[128,3584]{0,1:T(8,128)(2,1)}, u32[]{:S(2)}) copy-start(bf16[128,3584]{0,1:T(8,128)(2,1)} %all_gather.17) | copy-start | bytes 2752516
  154.5 6.7 %copy-start.5 = (bf16[2,64,3584]{2,1,0:T(8,128)(2,1)S(1)}, bf16[2,64,3584]{2,1,0:T(8,128)(2,1)}, u32[]{:S(2)}) copy-start(bf16[2,64,3584]{2,1,0:T(8,128)(2,1)} %all_to_all.57) | copy-start | bytes 2752516
  154.5 7.1 %copy-start.21 = (f32[128,2,64]{0,2,1:T(8,128)S(1)}, f32[128,2,64]{0,2,1:T(8,128)}, u32[]{:S(2)}) copy-start(f32[128,2,64]{0,2,1:T(8,128)} %fusion.9) | copy-start | bytes 196612
  154.5 87.8 %all-to-all-start.4 = ((bf16[8,2,28672]{2,1,0:T(2,128)(2,1)}), bf16[8,2,28672]{2,1,0:T(2,128)(2,1)}, u32[]{:S(2)}, u32[]{:S(2)}) async-start(bf16[8,2,28672]{2,1,0:T(2,128)(2,1)} %reshape.365), calls=%async_computation.4 | async-start | bytes 1835008 | tf_op jit(solution)/shard_map/all_to_all | solution.py:129
  161.2 1.0 copy-start.9
  161.2 1.1 copy-start.11
  162.3 31.3 %copy-start.7 = (bf16[1,512,448]{1,2,0:T(8,128)(2,1)S(1)}, bf16[1,512,448]{1,2,0:T(8,128)(2,1)}, u32[]{:S(2)}) copy-start(bf16[1,512,448]{1,2,0:T(8,128)(2,1)} %copy-done.6) | copy-start | bytes 1376260
  193.6 0.7 copy-start.14
  242.3 50.6 %all-to-all-start.1 = ((bf16[64,2,448]{2,1,0:T(2,128)(2,1)}), bf16[64,2,448]{2,1,0:T(2,128)(2,1)S(1)}, u32[]{:S(2)}, u32[]{:S(2)}) async-start(bf16[64,2,448]{2,1,0:T(2,128)(2,1)} %reshape.212), calls=%async_computation.1 | async-start | bytes 262144 | tf_op jit(solution)/shard_map/all_to_all | solution.py:103
  281.3 1.8 copy-start.3
  283.7 7.6 %copy-start.15 = (bf16[128,2,512]{0,2,1:T(8,128)(2,1)S(1)}, bf16[128,2,512]{0,2,1:T(8,128)(2,1)}, u32[]{:S(2)}) copy-start(bf16[128,2,512]{0,2,1:T(8,128)(2,1)} %copy-done.14) | copy-start | bytes 786436
  286.9 29.2 %collective-permute-start.3 = (bf16[64,3584]{1,0:T(8,128)(2,1)}, bf16[64,3584]{1,0:T(8,128)(2,1)}, u32[]{:S(2)}, u32[]{:S(2)}) collective-permute-start(bf16[64,3584]{1,0:T(8,128)(2,1)} %select_convert_fusion.2), channel_id=1, source_target_pairs={{0,8},{8,0},{16,24},{24,16},{32,40},{40,32},{48,56},{56,48},{64,72... | collective-permute-start | bytes 1376264 | tf_op jit(solution)/shard_map/ppermute | solution.py:14
  289.3 29.2 %collective-permute-start.4 = (bf16[64,3584]{1,0:T(8,128)(2,1)S(1)}, bf16[64,3584]{1,0:T(8,128)(2,1)}, u32[]{:S(2)}, u32[]{:S(2)}) collective-permute-start(bf16[64,3584]{1,0:T(8,128)(2,1)S(1)} %select_convert_fusion.1), channel_id=1, source_target_pairs={{0,8},{8,0},{16,24},{24,16},{32,40},{40,32},{48,56},{56,48},{64,72... | collective-permute-start | bytes 1376264 | tf_op jit(solution)/shard_map/ppermute | solution.py:14
  293.0 20.7 %all-to-all-start.6 = ((bf16[64,2,448]{2,1,0:T(2,128)(2,1)}), bf16[64,2,448]{2,1,0:T(2,128)(2,1)S(1)}, u32[]{:S(2)}, u32[]{:S(2)}) async-start(bf16[64,2,448]{2,1,0:T(2,128)(2,1)} %reshape.216), calls=%async_computation.6 | async-start | bytes 262144 | tf_op jit(solution)/shard_map/all_to_all | solution.py:138
  303.3 12.1 %copy-start.19 = (f32[12,8]{1,0:T(8,128)S(1)}, f32[12,8]{1,0:T(8,128)}, u32[]{:S(2)}) copy-start(f32[12,8]{1,0:T(8,128)} %copy-done.18) | copy-start | bytes 1156
  304.8 15.7 %collective-permute-start.5 = (bf16[512,448]{0,1:T(8,128)(2,1)S(1)}, bf16[512,448]{0,1:T(8,128)(2,1)}, u32[]{:S(2)}, u32[]{:S(2)}) collective-permute-start(bf16[512,448]{0,1:T(8,128)(2,1)S(1)} %select_convert_fusion), channel_id=1, source_target_pairs={{0,8},{8,0},{16,24},{24,16},{32,40},{40,32},{48,56},{56,48},{64,72... | collective-permute-start | bytes 1376264 | tf_op jit(solution)/shard_map/ppermute | solution.py:14
  318.6 2.0 copy-start.2
where the time goes:
time: 324 us; the launch traced here: 323 us
  blocking collectives  133 us (41%)
  starting transfers between devices  89.4 us (28%)
  local copies, waits for them, and re-layouts  50.9 us (16%)
  other arithmetic  19.4 us (6%)
  waiting for transfers between devices  18.9 us (6%)
  matrix products  9.43 us (3%)
    all_gather x1, blocking collectives, per_device(): full_rows = lax.all_gather(rows_part, 'replica', axis=1, tiled=True)  41.3 us
    all_gather x1, blocking collectives, per_device(): lax.all_gather(hidden, 'replica', axis=2, tiled=True)  30.9 us
    all_to_all x1, starting transfers between devices, per_device(): lax.all_to_all(expert_out.reshape(experts_axis, capacity, slice_width), '...  27.9 us
    all_gather x1, blocking collectives, per_device(): full_grads = lax.all_gather(grads_part, 'replica', axis=1, tiled=True)  24.1 us
    ppermute x6, starting transfers between devices, partner_2(): return lax.ppermute(block, axis, route)  19.9 us
    unnamed x50, local copies, waits for them, and re-layouts  18.8 us
    all_gather x1, blocking collectives, per_device(): lax.all_gather(gate_act, 'replica', axis=2, tiled=True)  18.8 us
    all_gather x1, blocking collectives, per_device(): lax.all_gather(up_act, 'replica', axis=2, tiled=True)  18.4 us
  transfers between devices with their start and end apart: 13, of which 3 were waited for; matrix products, arithmetic and copies ran while one was open for 22% of the time, Pallas kernels for 0%

commit v1 on v0

--- a/solution.py
+++ b/solution.py
@@ -121,8 +121,36 @@
     up_act = (hidden_grad * activated).astype(jnp.bfloat16)
     gate_local = jnp.einsum("sd,shq->hqd", full_rows, gate_act, preferred_element_type=jnp.float32)
     up_local = jnp.einsum("sd,shq->hqd", full_rows, up_act, preferred_element_type=jnp.float32)
+
+    def answer_shelves(v0):
+        left_arr, view_out, top = (lax.psum(1, "replica"), lax.axis_index("replica"), v0.shape[2])
+        panels = [pp * left_arr if hop_no == 2 else pp for hop_no, pp in enumerate(v0.shape)]
+        raw_out = lax.dynamic_update_slice_in_dim(
+            jnp.zeros(panels, v0.dtype), v0, view_out * top, axis=2
+        )
+        out_arr = e_now = v0
+        for ii in range(1, left_arr // 2 + 1):
+            out_arr = lax.ppermute(
+                out_arr,
+                "replica",
+                [(hop_no, (hop_no + 1) % left_arr) for hop_no in range(left_arr)],
+            )
+            raw_out = lax.dynamic_update_slice_in_dim(
+                raw_out, out_arr, (view_out - ii) % left_arr * top, axis=2
+            )
+            if 2 * ii < left_arr:
+                e_now = lax.ppermute(
+                    e_now,
+                    "replica",
+                    [(hop_no, (hop_no - 1) % left_arr) for hop_no in range(left_arr)],
+                )
+                raw_out = lax.dynamic_update_slice_in_dim(
+                    raw_out, e_now, (view_out + ii) % left_arr * top, axis=2
+                )
+        return raw_out
+
     all_gate_act, all_up_act = (
-        lax.all_gather(gate_act, "replica", axis=2, tiled=True),
+        answer_shelves(gate_act),
         lax.all_gather(up_act, "replica", axis=2, tiled=True),
     )
     rows_gate, rows_up = (

time: 324 us -> 323 us (level)
  blocking collectives: 133 us -> 101 us
  local copies, waits for them, and re-layouts: 50.9 us -> 72.7 us
  starting transfers between devices: 89.4 us -> 110 us
  waiting for transfers between devices: 18.9 us -> 8.68 us
    ppermute x0 -> x7, starting transfers between devices: none -> 22.6 us  [the longest x3 12.1 us: answer_shelves(): lax.ppermute(e_now, 'replica', [(hop_no, (hop_no - 1) % left_arr) for hop...]
    all_gather x1, blocking collectives: 41.3 us -> 21.4 us  [per_device(): full_rows = lax.all_gather(rows_part, 'replica', axis=1, tiled=True)]
    all_gather x1 -> x0, blocking collectives: 18.8 us -> none  [per_device(): lax.all_gather(gate_act, 'replica', axis=2, tiled=True)]
    all_to_all x1, starting transfers between devices: 27.9 us -> 10.2 us  [per_device(): lax.all_to_all(expert_out.reshape(experts_axis, capacity, slice_width), '...]
    ppermute x6, starting transfers between devices: 19.9 us -> 37.2 us  [partner_2(): return lax.ppermute(block, axis, route)]
    ppermute x0 -> x7, local copies, waits for them, and re-layouts: none -> 10.5 us  [the longest x4 5.98 us: answer_shelves(): lax.ppermute(out_arr, 'replica', [(hop_no, (hop_no + 1) % left_arr) for h...]
    dynamic_update_slice x0 -> x8, local copies, waits for them, and re-layouts: none -> 9.86 us  [the longest x4 4.89 us: answer_shelves(): lax.dynamic_update_slice_in_dim(raw_out, out_arr, (view_out - ii) % left_...]
    all_to_all x1, waiting for transfers between devices: 9.5 us -> 0.01 us  [per_device(): lax.all_to_all(send_rows.reshape(experts_axis, capacity, slice_width), 'e...]
  transfers between devices with their start and end apart: 13 -> 20, of which waited for: 3 -> 2; matrix products, arithmetic and copies ran while one was open for 22% -> 29% of each run, Pallas kernels for 0% -> 0%
where the time goes in v1:
time: 323 us; the launch traced here: 320 us
  starting transfers between devices  110 us (34%)
  blocking collectives  101 us (31%)
  local copies, waits for them, and re-layouts  72.7 us (23%)
  other arithmetic  17.3 us (5%)
  waiting for transfers between devices  8.68 us (3%)
  matrix products  8.39 us (3%)
    ppermute x6, starting transfers between devices, partner_2(): return lax.ppermute(block, axis, route)  37.2 us
    all_gather x1, blocking collectives, per_device(): lax.all_gather(up_act, 'replica', axis=2, tiled=True)  27.5 us
    all_gather x1, blocking collectives, per_device(): lax.all_gather(hidden, 'replica', axis=2, tiled=True)  27.3 us
    all_gather x1, blocking collectives, per_device(): full_grads = lax.all_gather(grads_part, 'replica', axis=1, tiled=True)  25.2 us
    all_gather x1, blocking collectives, per_device(): full_rows = lax.all_gather(rows_part, 'replica', axis=1, tiled=True)  21.4 us
    unnamed x42, local copies, waits for them, and re-layouts  19.1 us
    ppermute x3, starting transfers between devices, answer_shelves(): lax.ppermute(e_now, 'replica', [(hop_no, (hop_no - 1) % left_arr) for hop...  12.1 us
    another operation x3, local copies, waits for them, and re-layouts, pair_join(): return jnp.stack([first_part, second_part], axis=stack_axis)  10.7 us
  transfers between devices with their start and end apart: 20, of which 2 were waited for; matrix products, arithmetic and copies ran while one was open for 29% of the time, Pallas kernels for 0%

profile of v1, /device:TPU:1, one launch (start us, length us, event | category | flops | bytes accessed | tf_op | source)
XLA Modules:
  0.0 320.0 jit_solution(14434816095217856506)
XLA Ops:
  0.7 8.9 %collective-permute-start.2 = (bf16[512,448]{0,1:T(8,128)(2,1)}, bf16[512,448]{0,1:T(8,128)(2,1)S(1)}, u32[]{:S(2)}, u32[]{:S(2)}) collective-permute-start(bf16[512,448]{0,1:T(8,128)(2,1)} %bitcast.169), channel_id=1, source_target_pairs={{0,8},{8,0},{16,24},{24,16},{32,40},{40,32},{48,56},{56,48},{64,72... | collective-permute-start | bytes 1376264 | tf_op jit(solution)/shard_map/ppermute | solution.py:14
  13.2 1.2 gather_fusion.2
  15.4 8.1 %all-to-all-start.2 = ((bf16[64,2,448]{2,1,0:T(2,128)(2,1)}), bf16[64,2,448]{2,1,0:T(2,128)(2,1)S(1)}, u32[]{:S(2)}, u32[]{:S(2)}) async-start(bf16[64,2,448]{2,1,0:T(2,128)(2,1)} %select_convert_fusion.3), calls=%async_computation.2 | async-start | bytes 262144 | tf_op jit(solution)/shard_map/all_to_all | solution.py:63
  23.5 2.4 collective-permute-start.1
  25.9 2.0 collective-permute-start
  30.0 3.8 %all-to-all-done.2 = bf16[64,2,448]{2,1,0:T(2,128)(2,1)S(1)} async-done(((bf16[64,2,448]{2,1,0:T(2,128)(2,1)}), bf16[64,2,448]{2,1,0:T(2,128)(2,1)S(1)}, u32[]{:S(2)}, u32[]{:S(2)}) %all-to-all-start.2) | async-done | bytes 114720 | tf_op jit(solution)/shard_map/all_to_all | solution.py:63
  33.9 6.5 %all-to-all-start = ((bf16[64,2,448]{2,1,0:T(2,128)(2,1)}), bf16[64,2,448]{2,1,0:T(2,128)(2,1)S(1)}, u32[]{:S(2)}, u32[]{:S(2)}) async-start(bf16[64,2,448]{2,1,0:T(2,128)(2,1)} %broadcast_select_fusion), calls=%async_computation | async-start | bytes 262144 | tf_op jit(solution)/shard_map/all_to_all | solution.py:56
  40.6 25.2 %all_gather.14 = bf16[128,3584]{0,1:T(8,128)(2,1)} all-gather(bf16[128,448]{0,1:T(8,128)(2,1)S(1)} %copy.86), channel_id=1, replica_groups=mesh['expert'=64,'replica'=8] {'replica'}, dimensions={1}, use_global_device_ids=true | all-gather | bytes 1032192 | tf_op jit(solution)/shard_map/all_gather | solution.py:115
  66.0 21.4 %all_gather.12 = bf16[128,3584]{0,1:T(8,128)(2,1)S(1)} all-gather(bf16[128,448]{0,1:T(8,128)(2,1)S(1)} %copy.81), channel_id=1, replica_groups=mesh['expert'=64,'replica'=8] {'replica'}, dimensions={1}, use_global_device_ids=true | all-gather | bytes 1032192 | tf_op jit(solution)/shard_map/all_gather | solution.py:80
  87.7 2.1 copy.87
  89.7 4.2 %all-to-all-start.3 = ((bf16[2,512,448]{2,0,1:T(2,128)(2,1)}), bf16[2,512,448]{2,0,1:T(2,128)(2,1)}, u32[]{:S(2)}, u32[]{:S(2)}) async-start(bf16[2,512,448]{2,0,1:T(2,128)(2,1)} %copy.87), calls=%async_computation.3 | async-start | bytes 2097152 | tf_op jit(solution)/shard_map/all_to_all | solution.py:116
  94.0 1.2 select_bitcast_fusion.3
  96.2 1.0 pad_maximum_fusion.2
  97.2 4.3 %copy.101 = bf16[2,64,3584]{1,0,2:T(2,128)(2,1)S(1)} copy(bf16[2,64,3584]{2,1,0:T(8,128)(2,1)} %pad_maximum_fusion.2) | data formatting | bytes 1835008 | tf_op jit(solution)/shard_map/stack | solution.py:20
  101.5 2.1 reshape.363
  103.6 1.2 select_bitcast_fusion.5
  105.7 1.0 pad_maximum_fusion.1
  106.7 4.3 %copy.98 = bf16[2,64,3584]{1,0,2:T(2,128)(2,1)S(1)} copy(bf16[2,64,3584]{2,1,0:T(8,128)(2,1)} %pad_maximum_fusion.1) | data formatting | bytes 1835008 | tf_op jit(solution)/shard_map/stack | solution.py:20
  111.0 2.1 reshape.365
  113.2 1.5 fusion.9
  114.7 6.6 %all-to-all-start.5 = ((bf16[8,2,28672]{2,1,0:T(2,128)(2,1)}), bf16[8,2,28672]{2,1,0:T(2,128)(2,1)}, u32[]{:S(2)}, u32[]{:S(2)}) async-start(bf16[8,2,28672]{2,1,0:T(2,128)(2,1)} %reshape.363), calls=%async_computation.5 | async-start | bytes 1835008 | tf_op jit(solution)/shard_map/all_to_all | solution.py:158
  121.4 1.4 copy.88
  123.4 2.1 all_to_all.57
  125.5 1.9 fusion.3
  127.8 3.4 %collective-permute-start.3 = (bf16[128,2,64]{0,2,1:T(8,128)(2,1)S(1)}, bf16[128,2,64]{0,2,1:T(8,128)(2,1)S(1)}, u32[]{:S(2)}, u32[]{:S(2)}) collective-permute-start(bf16[128,2,64]{0,2,1:T(8,128)(2,1)S(1)} %get-tuple-element.59), channel_id=1, source_target_pairs={{0,1},{1,2},{2,3},{3,4},{4,5},{5,6},{6,7},{7,0},{8,9},{9,10},{10,1... | collective-permute-start | bytes 98312 | tf_op jit(solution)/shard_map/ppermute | solution.py:133
  131.2 3.1 collective-permute-start.4
  134.3 27.3 %all_gather.13 = bf16[128,2,512]{0,2,1:T(8,128)(2,1)} all-gather(bf16[128,2,64]{0,2,1:T(8,128)(2,1)S(1)} %get-tuple-element.61), channel_id=1, replica_groups=mesh['expert'=64,'replica'=8] {'replica'}, dimensions={2}, use_global_device_ids=true | all-gather | bytes 294912 | tf_op jit(solution)/shard_map/all_gather | solution.py:98
  164.2 4.4 %all-to-all-start.4 = ((bf16[8,2,28672]{2,1,0:T(2,128)(2,1)}), bf16[8,2,28672]{2,1,0:T(2,128)(2,1)}, u32[]{:S(2)}, u32[]{:S(2)}) async-start(bf16[8,2,28672]{2,1,0:T(2,128)(2,1)} %reshape.365), calls=%async_computation.4 | async-start | bytes 1835008 | tf_op jit(solution)/shard_map/all_to_all | solution.py:157
  168.6 1.7 fusion.16
  170.7 3.2 %collective-permute-start.5 = (bf16[128,2,64]{0,2,1:T(8,128)(2,1)S(1)}, bf16[128,2,64]{0,2,1:T(8,128)(2,1)S(1)}, u32[]{:S(2)}, u32[]{:S(2)}) collective-permute-start(bf16[128,2,64]{0,2,1:T(8,128)(2,1)S(1)} %collective-permute-done.3), channel_id=1, source_target_pairs={{0,1},{1,2},{2,3},{3,4},{4,5},{5,6},{6,7},{7,0},{8,9},{9,10},{10,1... | collective-permute-start | bytes 98312 | tf_op jit(solution)/shard_map/ppermute | solution.py:133
  173.9 27.5 %all_gather.15 = bf16[128,2,512]{0,2,1:T(8,128)(2,1)S(1)} all-gather(bf16[128,2,64]{0,2,1:T(8,128)(2,1)S(1)} %get-tuple-element.60), channel_id=1, replica_groups=mesh['expert'=64,'replica'=8] {'replica'}, dimensions={2}, use_global_device_ids=true | all-gather | bytes 294912 | tf_op jit(solution)/shard_map/all_gather | solution.py:154
  202.3 5.3 %reshape.364 = bf16[3584,2,64]{2,1,0:T(2,128)(2,1)} reshape(bf16[8,2,28672]{2,1,0:T(2,128)(2,1)} %all-to-all-done.5) | data formatting | bytes 1835008
  207.6 4.6 %copy.102 = bf16[2,64,8,448]{3,1,2,0:T(8,128)(2,1)S(1)} copy(bf16[2,64,8,448]{1,0,3,2:T(2,128)(2,1)} %bitcast.164) | data formatting | bytes 1835008 | tf_op jit(solution)/shard_map/all_to_all | solution.py:158
  212.2 19.4 %collective-permute-start.10 = (bf16[64,3584]{1,0:T(8,128)(2,1)}, bf16[64,3584]{1,0:T(8,128)(2,1)}, u32[]{:S(2)}, u32[]{:S(2)}) collective-permute-start(bf16[64,3584]{1,0:T(8,128)(2,1)} %select_convert_fusion.2), channel_id=1, source_target_pairs={{0,8},{8,0},{16,24},{24,16},{32,40},{40,32},{48,56},{56,48},{64,72... | collective-permute-start | bytes 1376264 | tf_op jit(solution)/shard_map/ppermute | solution.py:14
  231.6 4.1 %collective-permute-start.6 = (bf16[128,2,64]{0,2,1:T(8,128)(2,1)S(1)}, bf16[128,2,64]{0,2,1:T(8,128)(2,1)}, u32[]{:S(2)}, u32[]{:S(2)}) collective-permute-start(bf16[128,2,64]{0,2,1:T(8,128)(2,1)S(1)} %collective-permute-done.4), channel_id=1, source_target_pairs={{0,7},{1,0},{2,1},{3,2},{4,3},{5,4},{6,5},{7,6},{8,15},{9,8},{10,9... | collective-permute-start | bytes 98312 | tf_op jit(solution)/shard_map/ppermute | solution.py:142
  235.8 1.9 collective-permute-start.7
  238.6 2.2 collective-permute-start.11
  240.8 4.9 %collective-permute-start.8 = (bf16[128,2,64]{0,2,1:T(8,128)(2,1)}, bf16[128,2,64]{0,2,1:T(8,128)(2,1)}, u32[]{:S(2)}, u32[]{:S(2)}) collective-permute-start(bf16[128,2,64]{0,2,1:T(8,128)(2,1)} %collective-permute-done.6), channel_id=1, source_target_pairs={{0,7},{1,0},{2,1},{3,2},{4,3},{5,4},{6,5},{7,6},{8,15},{9,8},{10,9... | collective-permute-start | bytes 98312 | tf_op jit(solution)/shard_map/ppermute | solution.py:142
  245.7 1.9 collective-permute-start.9
  248.9 10.2 %all-to-all-start.1 = ((bf16[64,2,448]{2,1,0:T(2,128)(2,1)}), bf16[64,2,448]{2,1,0:T(2,128)(2,1)S(1)}, u32[]{:S(2)}, u32[]{:S(2)}) async-start(bf16[64,2,448]{2,1,0:T(2,128)(2,1)} %reshape.212), calls=%async_computation.1 | async-start | bytes 262144 | tf_op jit(solution)/shard_map/all_to_all | solution.py:103
  259.0 5.3 %reshape.366 = bf16[3584,2,64]{2,1,0:T(2,128)(2,1)} reshape(bf16[8,2,28672]{2,1,0:T(2,128)(2,1)} %all-to-all-done.4) | data formatting | bytes 1835008
  264.3 4.6 %copy.99 = bf16[2,64,8,448]{3,1,2,0:T(8,128)(2,1)S(1)} copy(bf16[2,64,8,448]{1,0,3,2:T(2,128)(2,1)} %bitcast.165) | data formatting | bytes 1835008 | tf_op jit(solution)/shard_map/all_to_all | solution.py:157
  269.0 1.1 dynamic_update_slice.24
  270.0 1.5 copy.91
  271.5 1.4 dynamic_update_slice.25
  272.9 1.5 copy.92
  274.4 1.4 dynamic_update_slice.26
  275.9 1.5 copy.93
  278.4 1.5 copy.94
  279.9 1.0 dynamic_update_slice.28
  280.9 1.5 copy.95
  282.4 1.4 dynamic_update_slice.29
  283.9 1.5 copy.96
  285.4 1.4 dynamic_update_slice.30
  286.8 1.5 copy.97
  288.3 1.0 dynamic_update_slice.31
  289.4 1.1 fusion.1
  292.2 10.3 %all-to-all-start.6 = ((bf16[64,2,448]{2,1,0:T(2,128)(2,1)}), bf16[64,2,448]{2,1,0:T(2,128)(2,1)S(1)}, u32[]{:S(2)}, u32[]{:S(2)}) async-start(bf16[64,2,448]{2,1,0:T(2,128)(2,1)} %reshape.216), calls=%async_computation.6 | async-start | bytes 262144 | tf_op jit(solution)/shard_map/all_to_all | solution.py:166
  302.5 1.5 select_convert_fusion
  304.1 2.4 collective-permute-start.12
  308.1 4.8 %all-to-all-done.6 = bf16[64,2,448]{2,1,0:T(2,128)(2,1)S(1)} async-done(((bf16[64,2,448]{2,1,0:T(2,128)(2,1)}), bf16[64,2,448]{2,1,0:T(2,128)(2,1)S(1)}, u32[]{:S(2)}, u32[]{:S(2)}) %all-to-all-start.6) | async-done | bytes 114720 | tf_op jit(solution)/shard_map/all_to_all | solution.py:166
  314.5 2.5 fusion.13
  316.9 2.0 fusion.14
  319.0 1.1 fusion.15
  (106 shorter events, 21.8 us)
Async XLA Ops:
  0.6 10.5 %copy-start = (bf16[12,448]{1,0:T(8,128)(2,1)S(1)}, bf16[12,448]{1,0:T(8,128)(2,1)}, u32[]{:S(2)}) copy-start(bf16[12,448]{1,0:T(8,128)(2,1)} %param.21) | copy-start | bytes 32260
  0.6 27.2 %copy-start.17 = (s32[12,8]{0,1:T(8,128)S(1)}, s32[12,8]{0,1:T(8,128)}, u32[]{:S(2)}) copy-start(s32[12,8]{0,1:T(8,128)} %param.16) | copy-start | bytes 1156
  0.7 27.3 %copy-start.1 = (bf16[12,448]{1,0:T(8,128)(2,1)S(1)}, bf16[12,448]{1,0:T(8,128)(2,1)}, u32[]{:S(2)}) copy-start(bf16[12,448]{1,0:T(8,128)(2,1)} %param.15) | copy-start | bytes 32260
  0.7 86.8 %collective-permute-start.2 = (bf16[512,448]{0,1:T(8,128)(2,1)}, bf16[512,448]{0,1:T(8,128)(2,1)S(1)}, u32[]{:S(2)}, u32[]{:S(2)}) collective-permute-start(bf16[512,448]{0,1:T(8,128)(2,1)} %bitcast.169), channel_id=1, source_target_pairs={{0,8},{8,0},{16,24},{24,16},{32,40},{40,32},{48,56},{56,48},{64,72... | collective-permute-start | bytes 1376264 | tf_op jit(solution)/shard_map/ppermute | solution.py:14
  15.4 18.4 %all-to-all-start.2 = ((bf16[64,2,448]{2,1,0:T(2,128)(2,1)}), bf16[64,2,448]{2,1,0:T(2,128)(2,1)S(1)}, u32[]{:S(2)}, u32[]{:S(2)}) async-start(bf16[64,2,448]{2,1,0:T(2,128)(2,1)} %select_convert_fusion.3), calls=%async_computation.2 | async-start | bytes 262144 | tf_op jit(solution)/shard_map/all_to_all | solution.py:63
  23.5 70.5 %collective-permute-start.1 = (bf16[64,3584]{1,0:T(8,128)(2,1)}, bf16[64,3584]{1,0:T(8,128)(2,1)}, u32[]{:S(2)}, u32[]{:S(2)}) collective-permute-start(bf16[64,3584]{1,0:T(8,128)(2,1)} %bitcast.6), channel_id=1, source_target_pairs={{0,8},{8,0},{16,24},{24,16},{32,40},{40,32},{48,56},{56,48},{64,72... | collective-permute-start | bytes 1376264 | tf_op jit(solution)/shard_map/ppermute | solution.py:14
  25.9 77.7 %collective-permute-start = (bf16[64,3584]{1,0:T(8,128)(2,1)}, bf16[64,3584]{1,0:T(8,128)(2,1)}, u32[]{:S(2)}, u32[]{:S(2)}) collective-permute-start(bf16[64,3584]{1,0:T(8,128)(2,1)} %bitcast.3), channel_id=1, source_target_pairs={{0,8},{8,0},{16,24},{24,16},{32,40},{40,32},{48,56},{56,48},{64,72... | collective-permute-start | bytes 1376264 | tf_op jit(solution)/shard_map/ppermute | solution.py:14
  28.9 58.5 %copy-start.13 = (bf16[1,512,448]{1,2,0:T(8,128)(2,1)S(1)}, bf16[1,512,448]{1,2,0:T(8,128)(2,1)}, u32[]{:S(2)}) copy-start(bf16[1,512,448]{1,2,0:T(8,128)(2,1)} %param.20) | copy-start | bytes 1376260
  33.9 31.9 %all-to-all-start = ((bf16[64,2,448]{2,1,0:T(2,128)(2,1)}), bf16[64,2,448]{2,1,0:T(2,128)(2,1)S(1)}, u32[]{:S(2)}, u32[]{:S(2)}) async-start(bf16[64,2,448]{2,1,0:T(2,128)(2,1)} %broadcast_select_fusion), calls=%async_computation | async-start | bytes 262144 | tf_op jit(solution)/shard_map/all_to_all | solution.py:56
  87.5 2.2 copy-start.4
  89.7 25.0 %all-to-all-start.3 = ((bf16[2,512,448]{2,0,1:T(2,128)(2,1)}), bf16[2,512,448]{2,0,1:T(2,128)(2,1)}, u32[]{:S(2)}, u32[]{:S(2)}) async-start(bf16[2,512,448]{2,0,1:T(2,128)(2,1)} %copy.87), calls=%async_computation.3 | async-start | bytes 2097152 | tf_op jit(solution)/shard_map/all_to_all | solution.py:116
  95.2 0.8 copy-start.10
  95.2 0.9 copy-start.11
  104.8 0.8 copy-start.6
  104.8 0.9 copy-start.8
  114.7 49.5 %all-to-all-start.5 = ((bf16[8,2,28672]{2,1,0:T(2,128)(2,1)}), bf16[8,2,28672]{2,1,0:T(2,128)(2,1)}, u32[]{:S(2)}, u32[]{:S(2)}) async-start(bf16[8,2,28672]{2,1,0:T(2,128)(2,1)} %reshape.363), calls=%async_computation.5 | async-start | bytes 1835008 | tf_op jit(solution)/shard_map/all_to_all | solution.py:158
  123.3 4.0 %copy-start.7 = (bf16[1,64,3584]{2,1,0:T(8,128)(2,1)S(1)}, bf16[1,64,3584]{2,1,0:T(8,128)(2,1)}, u32[]{:S(2)}) copy-start(bf16[1,64,3584]{2,1,0:T(8,128)(2,1)} %copy-done.6) | copy-start | bytes 1376260
  125.4 1.9 copy-start.9
  127.8 42.8 %collective-permute-start.3 = (bf16[128,2,64]{0,2,1:T(8,128)(2,1)S(1)}, bf16[128,2,64]{0,2,1:T(8,128)(2,1)S(1)}, u32[]{:S(2)}, u32[]{:S(2)}) collective-permute-start(bf16[128,2,64]{0,2,1:T(8,128)(2,1)S(1)} %get-tuple-element.59), channel_id=1, source_target_pairs={{0,1},{1,2},{2,3},{3,4},{4,5},{5,6},{6,7},{7,0},{8,9},{9,10},{10,1... | collective-permute-start | bytes 98312 | tf_op jit(solution)/shard_map/ppermute | solution.py:133
  131.2 100.4 %collective-permute-start.4 = (bf16[128,2,64]{0,2,1:T(8,128)(2,1)S(1)}, bf16[128,2,64]{0,2,1:T(8,128)(2,1)S(1)}, u32[]{:S(2)}, u32[]{:S(2)}) collective-permute-start(bf16[128,2,64]{0,2,1:T(8,128)(2,1)S(1)} %get-tuple-element.59), channel_id=1, source_target_pairs={{0,7},{1,0},{2,1},{3,2},{4,3},{5,4},{6,5},{7,6},{8,15},{9,8},{10,9... | collective-permute-start | bytes 98312 | tf_op jit(solution)/shard_map/ppermute | solution.py:142
  162.1 1.3 copy-start.2
  163.3 5.2 %copy-start.12 = (bf16[128,2,512]{0,2,1:T(8,128)(2,1)S(1)}, bf16[128,2,512]{0,2,1:T(8,128)(2,1)}, u32[]{:S(2)}) copy-start(bf16[128,2,512]{0,2,1:T(8,128)(2,1)} %all_gather.13) | copy-start | bytes 786436
  164.2 6.1 %copy-start.5 = (bf16[1,512,448]{1,2,0:T(8,128)(2,1)S(1)}, bf16[1,512,448]{1,2,0:T(8,128)(2,1)}, u32[]{:S(2)}) copy-start(bf16[1,512,448]{1,2,0:T(8,128)(2,1)} %copy-done.4) | copy-start | bytes 1376260
  164.2 84.7 %all-to-all-start.4 = ((bf16[8,2,28672]{2,1,0:T(2,128)(2,1)}), bf16[8,2,28672]{2,1,0:T(2,128)(2,1)}, u32[]{:S(2)}, u32[]{:S(2)}) async-start(bf16[8,2,28672]{2,1,0:T(2,128)(2,1)} %reshape.365), calls=%async_computation.4 | async-start | bytes 1835008 | tf_op jit(solution)/shard_map/all_to_all | solution.py:157
  170.7 41.5 %copy-start.15 = (bf16[128,2,64]{0,2,1:T(8,128)(2,1)}, bf16[128,2,64]{0,2,1:T(8,128)(2,1)S(1)}, u32[]{:S(2)}) copy-start(bf16[128,2,64]{0,2,1:T(8,128)(2,1)S(1)} %collective-permute-done.3) | copy-start | bytes 98308
  170.7 65.1 %collective-permute-start.5 = (bf16[128,2,64]{0,2,1:T(8,128)(2,1)S(1)}, bf16[128,2,64]{0,2,1:T(8,128)(2,1)S(1)}, u32[]{:S(2)}, u32[]{:S(2)}) collective-permute-start(bf16[128,2,64]{0,2,1:T(8,128)(2,1)S(1)} %collective-permute-done.3), channel_id=1, source_target_pairs={{0,1},{1,2},{2,3},{3,4},{4,5},{5,6},{6,7},{7,0},{8,9},{9,10},{10,1... | collective-permute-start | bytes 98312 | tf_op jit(solution)/shard_map/ppermute | solution.py:133
  212.2 102.3 %collective-permute-start.10 = (bf16[64,3584]{1,0:T(8,128)(2,1)}, bf16[64,3584]{1,0:T(8,128)(2,1)}, u32[]{:S(2)}, u32[]{:S(2)}) collective-permute-start(bf16[64,3584]{1,0:T(8,128)(2,1)} %select_convert_fusion.2), channel_id=1, source_target_pairs={{0,8},{8,0},{16,24},{24,16},{32,40},{40,32},{48,56},{56,48},{64,72... | collective-permute-start | bytes 1376264 | tf_op jit(solution)/shard_map/ppermute | solution.py:14
  231.6 17.2 %copy-start.14 = (bf16[128,2,64]{0,2,1:T(8,128)(2,1)}, bf16[128,2,64]{0,2,1:T(8,128)(2,1)S(1)}, u32[]{:S(2)}) copy-start(bf16[128,2,64]{0,2,1:T(8,128)(2,1)S(1)} %collective-permute-done.4) | copy-start | bytes 98308
  231.6 9.1 %collective-permute-start.6 = (bf16[128,2,64]{0,2,1:T(8,128)(2,1)S(1)}, bf16[128,2,64]{0,2,1:T(8,128)(2,1)}, u32[]{:S(2)}, u32[]{:S(2)}) collective-permute-start(bf16[128,2,64]{0,2,1:T(8,128)(2,1)S(1)} %collective-permute-done.4), channel_id=1, source_target_pairs={{0,7},{1,0},{2,1},{3,2},{4,3},{5,4},{6,5},{7,6},{8,15},{9,8},{10,9... | collective-permute-start | bytes 98312 | tf_op jit(solution)/shard_map/ppermute | solution.py:142
  235.8 13.1 %copy-start.16 = (bf16[128,2,64]{0,2,1:T(8,128)(2,1)}, bf16[128,2,64]{0,2,1:T(8,128)(2,1)S(1)}, u32[]{:S(2)}) copy-start(bf16[128,2,64]{0,2,1:T(8,128)(2,1)S(1)} %collective-permute-done.5) | copy-start | bytes 98308
  235.8 9.9 %collective-permute-start.7 = (bf16[128,2,64]{0,2,1:T(8,128)(2,1)S(1)}, bf16[128,2,64]{0,2,1:T(8,128)(2,1)}, u32[]{:S(2)}, u32[]{:S(2)}) collective-permute-start(bf16[128,2,64]{0,2,1:T(8,128)(2,1)S(1)} %collective-permute-done.5), channel_id=1, source_target_pairs={{0,1},{1,2},{2,3},{3,4},{4,5},{5,6},{6,7},{7,0},{8,9},{9,10},{10,1... | collective-permute-start | bytes 98312 | tf_op jit(solution)/shard_map/ppermute | solution.py:133
  238.6 78.4 %collective-permute-start.11 = (bf16[64,3584]{1,0:T(8,128)(2,1)}, bf16[64,3584]{1,0:T(8,128)(2,1)}, u32[]{:S(2)}, u32[]{:S(2)}) collective-permute-start(bf16[64,3584]{1,0:T(8,128)(2,1)} %select_convert_fusion.1), channel_id=1, source_target_pairs={{0,8},{8,0},{16,24},{24,16},{32,40},{40,32},{48,56},{56,48},{64,72... | collective-permute-start | bytes 1376264 | tf_op jit(solution)/shard_map/ppermute | solution.py:14
  240.8 43.1 %collective-permute-start.8 = (bf16[128,2,64]{0,2,1:T(8,128)(2,1)}, bf16[128,2,64]{0,2,1:T(8,128)(2,1)}, u32[]{:S(2)}, u32[]{:S(2)}) collective-permute-start(bf16[128,2,64]{0,2,1:T(8,128)(2,1)} %collective-permute-done.6), channel_id=1, source_target_pairs={{0,7},{1,0},{2,1},{3,2},{4,3},{5,4},{6,5},{7,6},{8,15},{9,8},{10,9... | collective-permute-start | bytes 98312 | tf_op jit(solution)/shard_map/ppermute | solution.py:142
  245.7 41.2 %collective-permute-start.9 = (bf16[128,2,64]{0,2,1:T(8,128)(2,1)}, bf16[128,2,64]{0,2,1:T(8,128)(2,1)}, u32[]{:S(2)}, u32[]{:S(2)}) collective-permute-start(bf16[128,2,64]{0,2,1:T(8,128)(2,1)} %collective-permute-done.7), channel_id=1, source_target_pairs={{0,1},{1,2},{2,3},{3,4},{4,5},{5,6},{6,7},{7,0},{8,9},{9,10},{10,1... | collective-permute-start | bytes 98312 | tf_op jit(solution)/shard_map/ppermute | solution.py:133
  248.9 43.4 %all-to-all-start.1 = ((bf16[64,2,448]{2,1,0:T(2,128)(2,1)}), bf16[64,2,448]{2,1,0:T(2,128)(2,1)S(1)}, u32[]{:S(2)}, u32[]{:S(2)}) async-start(bf16[64,2,448]{2,1,0:T(2,128)(2,1)} %reshape.212), calls=%async_computation.1 | async-start | bytes 262144 | tf_op jit(solution)/shard_map/all_to_all | solution.py:103
  292.2 20.7 %all-to-all-start.6 = ((bf16[64,2,448]{2,1,0:T(2,128)(2,1)}), bf16[64,2,448]{2,1,0:T(2,128)(2,1)S(1)}, u32[]{:S(2)}, u32[]{:S(2)}) async-start(bf16[64,2,448]{2,1,0:T(2,128)(2,1)} %reshape.216), calls=%async_computation.6 | async-start | bytes 262144 | tf_op jit(solution)/shard_map/all_to_all | solution.py:166
  304.1 14.9 %collective-permute-start.12 = (bf16[512,448]{0,1:T(8,128)(2,1)S(1)}, bf16[512,448]{0,1:T(8,128)(2,1)S(1)}, u32[]{:S(2)}, u32[]{:S(2)}) collective-permute-start(bf16[512,448]{0,1:T(8,128)(2,1)S(1)} %select_convert_fusion), channel_id=1, source_target_pairs={{0,8},{8,0},{16,24},{24,16},{32,40},{40,32},{48,56},{56,48},{64,72... | collective-permute-start | bytes 1376264 | tf_op jit(solution)/shard_map/ppermute | solution.py:14
  316.9 2.0 copy-start.3
